TPU v7x, 512 devices: a whole 4x4x16 slice. The times are simulated.
512 devices in a mesh: wide: 32 (over z, core), narrow: 16 (over x, y).
Axes of the slice: x: 4, y: 4, z: 16, core: 2. Of those that a mesh axis runs over, the one named last changes fastest.
Arguments:
- activations: bfloat16 [512, 16384], P(None, 'wide'), may hold values from -6 to 6
- enc_weight: bfloat16 [16384, 16384], P('wide', 'narrow'), may hold values from -0.046875 to 0.046875
- enc_bias: float32 [16384], P('narrow'), may hold values from -4 to 4
- dec_weight: bfloat16 [16384, 16384], P('narrow', 'wide'), may hold values from -0.375 to 0.375
- dec_bias: float32 [16384], P('wide'), may hold values from -4 to 4
- active_ids: int32 [512, 64], replicated, may hold values from 0 to 16383, all different within a row
Outputs:
- dec_grad: bfloat16 [16384, 16384], P('narrow', 'wide')
- latent_grad: float32 [512, 16384], P('wide', 'narrow')
Inputs may be any that keep to these rules, and one draw needn't show every extreme that they name: `active_ids`: each row names 64 different latents; every latent is named by some row.
All inputs are finite; a program needn't handle non-finite values.
Results may differ from a plain program's by a relative error of at most 0.0058.
Values may be sent and summed in bfloat16 or wider, within the bound.
No kernel may reach another device: no remote copies, remote signals or barrier semaphores. Data moves between devices by JAX's collectives and lax.ppermute only.
A program may use at most 128 MiB of HBM per device.

v0:
```python
import jax
import jax.numpy as jnp
from jax import lax
from jax.sharding import Mesh
from jax.sharding import PartitionSpec as P

NARROW = ("narrow_0", "narrow_1")
WIDE = ("wide_0", "wide_1")


def filled_with(value, identity):
    return jnp.broadcast_to(jnp.asarray(identity, value.dtype), value.shape)


def carried_in(value, axes, combine, identity, reverse):
    before = start = filled_with(value, identity)
    total = value
    for axis in reversed(axes):
        length, position = (lax.axis_size(axis), lax.axis_index(axis))
        pieces = lax.all_gather(total, axis)
        inside, total = (start, start)
        for k in reversed(range(length)) if reverse else range(length):
            passed = k > position if reverse else k < position
            total = combine(total, pieces[k])
            inside = jnp.where(passed, total, inside)
        before = combine(inside, before)
    return before


def reduced_to_own(pieces, axes, turns):
    inside = pieces.shape[1:]
    pieces = pieces.reshape(*(lax.axis_size(a) for a in axes), *inside)
    pieces = jnp.moveaxis(pieces, turns, range(len(axes))).reshape(-1, *inside)
    for k in turns:
        pieces = lax.psum_scatter(pieces, axes[k], scatter_dimension=0, tiled=True)
    return pieces[0]


def in_blocks(value, dim, length):
    dims = value.shape
    pieces = value.reshape(*dims[:dim], length, dims[dim] // length, *dims[dim + 1 :])
    return jnp.moveaxis(pieces, dim, 0)


def summed_rows(value, axes, turns, dim):
    length = lax.axis_size(axes)
    return reduced_to_own(in_blocks(value, dim, length), axes, turns)


def add_fields(earlier, later):
    return jax.tree.map(jnp.add, earlier, later)


def local(activations, enc_weight, enc_bias, dec_weight, dec_bias, active_ids):
    token_count = activations.shape[0]
    latent_width = enc_weight.shape[1]
    groups = lax.axis_size(NARROW)
    group_index = lax.axis_index(NARROW)
    first_latent = group_index * latent_width
    inside = (active_ids >= first_latent) & (active_ids < first_latent + latent_width)
    local_ids = jnp.where(inside, active_ids - first_latent, latent_width)
    row_index = jnp.arange(token_count, dtype=jnp.int32)[:, None]
    active_mask = (
        jnp.zeros((token_count, latent_width), jnp.float32)
        .at[row_index, local_ids]
        .set(1.0, mode="drop")
    )
    share_rows = token_count // lax.axis_size(WIDE)
    offset = lax.axis_index(WIDE) * share_rows
    own_mask = lax.dynamic_slice_in_dim(active_mask, offset, share_rows, 0)
    partial_pre = jnp.dot(activations, enc_weight, preferred_element_type=jnp.float32)
    preact = lax.psum(partial_pre, WIDE) + enc_bias
    latents = (active_mask * preact).astype(jnp.bfloat16)
    recon_part = jnp.dot(latents, dec_weight, preferred_element_type=jnp.float32)
    target = activations.astype(jnp.float32)
    nothing = jnp.zeros_like(recon_part)
    before = carried_in(recon_part, NARROW, add_fields, nothing, False)
    errors_here = dec_bias + before + recon_part - target
    later_sum = carried_in(errors_here, NARROW, add_fields, nothing, True)
    suffix = later_sum + errors_here
    errors = (suffix / groups).astype(jnp.bfloat16)
    dec_grad = lax.dot_general(
        latents, errors, (((0,), (0,)), ((), ())), preferred_element_type=jnp.float32
    ).astype(jnp.bfloat16)
    latent_rows = summed_rows(
        lax.dot_general(
            errors, dec_weight, (((1,), (1,)), ((), ())), preferred_element_type=jnp.float32
        ),
        WIDE,
        (1, 0),
        0,
    )
    latent_out = own_mask * latent_rows
    return (dec_grad, latent_out)


def solution(mesh):
    split = Mesh(mesh.devices.reshape(16, 2, 4, 4), ("wide_0", "wide_1", "narrow_0", "narrow_1"))
    return jax.shard_map(
        local,
        mesh=split,
        in_specs=(P(None, WIDE), P(WIDE, NARROW), P(NARROW), P(NARROW, WIDE), P(WIDE), P()),
        out_specs=(P(NARROW, WIDE), P(WIDE, NARROW)),
        check_vma=False,
    )
```

profile of v0, /device:TPU:2, one launch (start us, length us, event | category | flops | bytes accessed | tf_op | source)
XLA Modules:
  0.0 583.1 jit_solution(8263159260602203690)
XLA Ops:
  7.2 0.0 copy-start
  7.2 0.0 copy-start.7
  7.2 0.0 all-reduce.2.cloned.1.call-start
  7.2 3.5 fusion.17
  10.8 0.0 all-reduce.2.cloned.1.call-update
  10.8 0.0 all-gather.11.cloned.1.call-start
  10.9 0.5 copy-done.11
  11.4 0.1 multiply_reduce_fusion
  11.5 0.1 and_reduce_fusion
  11.7 0.1 copy.10
  11.8 0.1 reshape.66
  11.9 121.5 %scatter_custom_fusion = f32[524288]{0:T(1024)} fusion(s32[32768]{0:T(1024)S(1)} %reshape.66, f32[32768]{0:T(1024)S(1)} %broadcast.52, f32[]{:T(128)} %constant.17.clone.1), kind=kCustom, calls=%fused_computation.31 | custom fusion | bytes 2097156
  133.4 1.7 reshape.63
  135.1 94.1 %all-reduce.2.cloned.1.call-done = f32[512,1024]{1,0:T(8,128)} async-done(((f32[512,1024]{1,0:T(8,128)}), f32[512,1024]{1,0:T(8,128)}) %all-reduce.2.cloned.1.call-update) | async-done | bytes 2097168 | tf_op jit(solution)/shard_map/psum | solution.py:72
  229.2 2.1 multiply_convert_fusion
  231.3 0.0 copy-start.5
  231.3 1.0 copy-done.5
  232.3 1.7 fusion.18
  234.0 0.0 all-gather.11.cloned.1.call-update
  234.0 0.0 copy-start.4
  234.0 0.0 copy-start.9
  234.0 0.0 all-gather.7.cloned.1.call-start
  234.1 56.1 %all-gather.11.cloned.1.call-done = f32[2048,512]{1,0:T(8,128)} async-done(((f32[512,512]{1,0:T(8,128)}), f32[2048,512]{1,0:T(8,128)}) %all-gather.11.cloned.1.call-update) | async-done | bytes 4194320 | tf_op jit(solution)/shard_map/all_gather | solution.py:20
  290.1 3.7 fusion.13
  293.8 0.0 all-gather.7.cloned.1.call-update
  293.8 0.0 all-gather.13.cloned.1.call-start
  293.9 55.8 %all-gather.7.cloned.1.call-done = f32[4,512,512]{2,1,0:T(8,128)} async-done(((f32[1,512,512]{2,1,0:T(8,128)}), f32[4,512,512]{2,1,0:T(8,128)}) %all-gather.7.cloned.1.call-update) | async-done | bytes 4194320 | tf_op jit(solution)/shard_map/all_gather | solution.py:20
  349.7 0.0 copy-done.3
  349.7 5.6 fusion.12
  355.3 0.0 all-gather.13.cloned.1.call-update
  355.3 0.0 all-gather.9.cloned.1.call-start
  355.4 57.1 %all-gather.13.cloned.1.call-done = f32[2048,512]{1,0:T(8,128)} async-done(((f32[512,512]{1,0:T(8,128)}), f32[2048,512]{1,0:T(8,128)}) %all-gather.13.cloned.1.call-update) | async-done | bytes 4194320 | tf_op jit(solution)/shard_map/all_gather | solution.py:20
  412.5 3.7 fusion.6
  416.1 0.0 all-gather.9.cloned.1.call-update
  416.2 0.0 reduce-scatter.3.cloned.1.call-start
  416.2 55.8 %all-gather.9.cloned.1.call-done = f32[4,512,512]{2,1,0:T(8,128)} async-done(((f32[1,512,512]{2,1,0:T(8,128)}), f32[4,512,512]{2,1,0:T(8,128)}) %all-gather.9.cloned.1.call-update) | async-done | bytes 4194320 | tf_op jit(solution)/shard_map/all_gather | solution.py:20
  472.0 0.0 copy-done.1
  472.0 4.6 fusion.5
  476.6 0.7 fusion.19
  477.4 1.5 copy.11
  478.8 0.0 reduce-scatter.3.cloned.1.call-update
  478.9 0.0 reduce-scatter.5.cloned.1.call-start
  478.9 21.2 %reduce-scatter.3.cloned.1.call-done = f32[16,16,1024]{2,1,0:T(8,128)} async-done(((f32[32,16,1024]{2,1,0:T(8,128)}), f32[16,16,1024]{2,1,0:T(8,128)}) %reduce-scatter.3.cloned.1.call-update) | async-done | bytes 1048592 | tf_op jit(solution)/shard_map/reduce_scatter | solution.py:35
  500.1 0.0 reduce-scatter.5.cloned.1.call-update
  500.2 0.0 copy-done.6
  500.2 1.7 convolution_convert_fusion
  501.9 72.8 %reduce-scatter.5.cloned.1.call-done = f32[1,16,1024]{2,1,0:T(8,128)} async-done(((f32[16,16,1024]{2,1,0:T(8,128)}), f32[1,16,1024]{2,1,0:T(8,128)}) %reduce-scatter.5.cloned.1.call-update) | async-done | bytes 65552 | tf_op jit(solution)/shard_map/reduce_scatter | solution.py:35
  574.7 1.5 bitcast_multiply_fusion
  (18 shorter events, 0.1 us)
Async XLA Ops:
  7.2 225.1 %copy-start = (bf16[1024,512]{1,0:T(8,128)(2,1)S(1)}, bf16[1024,512]{1,0:T(8,128)(2,1)}, u32[]{:S(2)}) copy-start(bf16[1024,512]{1,0:T(8,128)(2,1)} %param.9) | copy-start | bytes 3145732
  7.2 3.7 copy-start.7
  7.2 222.0 %all-reduce.2.cloned.1.call-start = ((), (), s32[]{:S(2)}) async-start(), calls=%async_computation.2 | async-start | bytes 4194304 | tf_op jit(solution)/shard_map/psum | solution.py:72
  10.8 0.7 copy-start.11
  10.8 0.7 copy-start.10
  10.8 279.3 %all-gather.11.cloned.1.call-start = ((), (), s32[]{:S(2)}) async-start(), calls=%async_computation.7 | async-start | bytes 5242880 | tf_op jit(solution)/shard_map/all_gather | solution.py:20
  133.4 95.8 %copy-start.8 = (f32[1024]{0:T(1024)S(1)}, f32[1024]{0:T(1024)}, u32[]{:S(2)}) copy-start(f32[1024]{0:T(1024)} %param.8) | copy-start | bytes 12292
  135.1 96.2 %copy-start.2 = (f32[512,1024]{1,0:T(8,128)}, f32[512,1024]{1,0:T(8,128)S(1)}, u32[]{:S(2)}) copy-start(f32[512,1024]{1,0:T(8,128)S(1)} %reshape.63) | copy-start | bytes 6291460
  231.3 1.0 copy-start.5
  234.0 115.7 %copy-start.3 = (f32[512,512]{1,0:T(8,128)S(1)}, f32[512,512]{1,0:T(8,128)}, u32[]{:S(2)}) copy-start(f32[512,512]{1,0:T(8,128)} %fusion.18) | copy-start | bytes 3145732
  234.0 115.7 %copy-start.4 = (bf16[512,512]{1,0:T(8,128)(2,1)S(1)}, bf16[512,512]{1,0:T(8,128)(2,1)}, u32[]{:S(2)}) copy-start(bf16[512,512]{1,0:T(8,128)(2,1)} %param.6) | copy-start | bytes 1572868
  234.0 115.7 %copy-start.9 = (f32[512]{0:T(512)S(1)}, f32[512]{0:T(512)}, u32[]{:S(2)}) copy-start(f32[512]{0:T(512)} %param.10) | copy-start | bytes 6148
  234.0 115.6 %all-gather.7.cloned.1.call-start = ((), (), s32[]{:S(2)}) async-start(), calls=%async_computation.3 | async-start | bytes 5242880 | tf_op jit(solution)/shard_map/all_gather | solution.py:20
  293.8 118.7 %all-gather.13.cloned.1.call-start = ((), (), s32[]{:S(2)}) async-start(), calls=%async_computation.8 | async-start | bytes 5242880 | tf_op jit(solution)/shard_map/all_gather | solution.py:20
  355.3 116.7 %copy-start.1 = (f32[512,512]{1,0:T(8,128)S(1)}, f32[512,512]{1,0:T(8,128)}, u32[]{:S(2)}) copy-start(f32[512,512]{1,0:T(8,128)} %fusion.12) | copy-start | bytes 3145732
  355.3 116.7 %all-gather.9.cloned.1.call-start = ((), (), s32[]{:S(2)}) async-start(), calls=%async_computation.4 | async-start | bytes 5242880 | tf_op jit(solution)/shard_map/all_gather | solution.py:20
  416.2 84.0 %reduce-scatter.3.cloned.1.call-start = ((), (), s32[]{:S(2)}) async-start(), calls=%async_computation.5 | async-start | bytes 3145728 | tf_op jit(solution)/shard_map/reduce_scatter | solution.py:35
  478.8 21.3 %copy-start.6 = (bf16[512,1024]{1,0:T(8,128)(2,1)S(1)}, bf16[512,1024]{1,0:T(8,128)(2,1)}, u32[]{:S(2)}) copy-start(bf16[512,1024]{1,0:T(8,128)(2,1)} %copy-done.5) | copy-start | bytes 3145732
  478.9 95.9 %reduce-scatter.5.cloned.1.call-start = ((), (), s32[]{:S(2)}) async-start(), calls=%async_computation.6 | async-start | bytes 1114112 | tf_op jit(solution)/shard_map/reduce_scatter | solution.py:35
Sparse Core Ops, SparseCore 0:
  10.9 218.2 all-reduce.1
  234.1 55.9 all-gather.10
  293.9 55.6 all-gather.6
  355.4 57.0 all-gather.12
  416.3 55.6 all-gather.8
  479.0 21.1 reduce-scatter.2
  502.9 71.7 reduce-scatter.4
where the time goes:
time: 583 us
  waiting for transfers between devices  413 us (71%)
  local copies, waits for them, and re-layouts  126 us (22%)
  other arithmetic  21.4 us (4%)
  between operations  14.3 us (2%)
  matrix products  7.66 us (1%)
    all_gather x4, waiting for transfers between devices, carried_in(): pieces = lax.all_gather(total, axis)  225 us
    unnamed x28, local copies, waits for them, and re-layouts  123 us
    reduce_scatter x2, waiting for transfers between devices, reduced_to_own(): pieces = lax.psum_scatter(pieces, axes[k], scatter_dimension=0, tiled=True)  94.1 us
    psum x1, waiting for transfers between devices, local(): preact = lax.psum(partial_pre, WIDE) + enc_bias  94.1 us
  transfers between devices with their start and end apart: 7, of which 7 were waited for; matrix products, arithmetic and copies ran while one was open for 22% of the time, Pallas kernels for 0%

commit v1 on v0

--- a/solution.py
+++ b/solution.py
@@ -69,7 +69,7 @@
     offset = lax.axis_index(WIDE) * share_rows
     own_mask = lax.dynamic_slice_in_dim(active_mask, offset, share_rows, 0)
     partial_pre = jnp.dot(activations, enc_weight, preferred_element_type=jnp.float32)
-    preact = lax.psum(partial_pre, WIDE) + enc_bias
+    preact = jnp.sum(lax.all_gather(partial_pre, WIDE), axis=0) + enc_bias
     latents = (active_mask * preact).astype(jnp.bfloat16)
     recon_part = jnp.dot(latents, dec_weight, preferred_element_type=jnp.float32)
     target = activations.astype(jnp.float32)

time: 583 us -> 750 us (1.29)
  the two profiles are of different devices: /device:TPU:2 before, /device:TPU:4 now
where the time goes in v1:
time: 750 us
  waiting for transfers between devices  557 us (74%)
  local copies, waits for them, and re-layouts  126 us (17%)
  other arithmetic  43.6 us (6%)
  between operations  14.3 us (2%)
  matrix products  7.78 us (1%)
    all_gather x1, waiting for transfers between devices, local(): preact = jnp.sum(lax.all_gather(partial_pre, WIDE), axis=0) + enc_bias  240 us
    all_gather x4, waiting for transfers between devices, carried_in(): pieces = lax.all_gather(total, axis)  222 us
    unnamed x28, local copies, waits for them, and re-layouts  123 us
    reduce_scatter x2, waiting for transfers between devices, reduced_to_own(): pieces = lax.psum_scatter(pieces, axes[k], scatter_dimension=0, tiled=True)  94.6 us
    reduce_sum x1, other arithmetic, local(): preact = jnp.sum(lax.all_gather(partial_pre, WIDE), axis=0) + enc_bias  22.2 us
  transfers between devices with their start and end apart: 7, of which 7 were waited for; matrix products, arithmetic and copies ran while one was open for 17% of the time, Pallas kernels for 0%

profile of v1, /device:TPU:4, one launch (start us, length us, event | category | flops | bytes accessed | tf_op | source)
XLA Modules:
  0.0 749.8 jit_solution(4290130528920797497)
XLA Ops:
  7.2 0.0 copy-start
  7.2 0.0 all-gather.13.cloned.1.call-start
  7.2 3.6 fusion.17
  10.8 0.0 all-gather.13.cloned.1.call-update
  10.8 0.0 all-gather.15.cloned.1.call-start
  11.0 0.5 copy-done.11
  11.4 0.1 multiply_reduce_fusion
  11.5 0.1 and_reduce_fusion
  11.7 0.1 copy.10
  11.8 0.1 reshape.66
  11.9 121.5 %scatter_custom_fusion = f32[524288]{0:T(1024)} fusion(s32[32768]{0:T(1024)S(1)} %reshape.66, f32[32768]{0:T(1024)S(1)} %broadcast.52, f32[]{:T(128)} %constant.17.clone.1), kind=kCustom, calls=%fused_computation.31 | custom fusion | bytes 2097156
  133.4 1.8 reshape.63
  135.2 0.0 copy-start.2
  135.2 240.3 %all-gather.13.cloned.1.call-done = f32[16384,1024]{1,0:T(8,128)} async-done(((f32[512,1024]{1,0:T(8,128)}), f32[16384,1024]{1,0:T(8,128)}) %all-gather.13.cloned.1.call-update) | async-done | bytes 67108880 | tf_op jit(solution)/shard_map/all_gather | solution.py:72
  375.5 22.2 %reduce_sum.9 = f32[512,1024]{1,0:T(8,128)} reduce(f32[32,512,1024]{2,1,0:T(8,128)} %bitcast.1, f32[]{:T(128)} %constant.17.clone.1), dimensions={0}, to_apply=%region_1.2 | reduce | flops 16252928 | bytes 69206016 | tf_op jit(solution)/shard_map/reduce_sum | solution.py:72
  397.7 0.0 copy-done.2
  397.7 2.1 multiply_convert_fusion
  399.8 0.0 copy-start.5
  399.8 1.0 copy-done.5
  400.7 1.8 fusion.18
  402.5 0.0 all-gather.15.cloned.1.call-update
  402.5 0.0 copy-start.4
  402.6 0.0 copy-start.9
  402.6 0.0 all-gather.9.cloned.1.call-start
  402.6 53.9 %all-gather.15.cloned.1.call-done = f32[2048,512]{1,0:T(8,128)} async-done(((f32[512,512]{1,0:T(8,128)}), f32[2048,512]{1,0:T(8,128)}) %all-gather.15.cloned.1.call-update) | async-done | bytes 4194320 | tf_op jit(solution)/shard_map/all_gather | solution.py:20
  456.6 3.6 fusion.13
  460.2 0.0 all-gather.9.cloned.1.call-update
  460.2 0.0 all-gather.17.cloned.1.call-start
  460.3 55.5 %all-gather.9.cloned.1.call-done = f32[4,512,512]{2,1,0:T(8,128)} async-done(((f32[1,512,512]{2,1,0:T(8,128)}), f32[4,512,512]{2,1,0:T(8,128)}) %all-gather.9.cloned.1.call-update) | async-done | bytes 4194320 | tf_op jit(solution)/shard_map/all_gather | solution.py:20
  515.8 5.7 fusion.12
  521.5 0.0 all-gather.17.cloned.1.call-update
  521.5 0.0 all-gather.11.cloned.1.call-start
  521.6 57.4 %all-gather.17.cloned.1.call-done = f32[2048,512]{1,0:T(8,128)} async-done(((f32[512,512]{1,0:T(8,128)}), f32[2048,512]{1,0:T(8,128)}) %all-gather.17.cloned.1.call-update) | async-done | bytes 4194320 | tf_op jit(solution)/shard_map/all_gather | solution.py:20
  579.0 3.6 fusion.6
  582.6 0.0 all-gather.11.cloned.1.call-update
  582.6 0.0 reduce-scatter.3.cloned.1.call-start
  582.7 55.5 %all-gather.11.cloned.1.call-done = f32[4,512,512]{2,1,0:T(8,128)} async-done(((f32[1,512,512]{2,1,0:T(8,128)}), f32[4,512,512]{2,1,0:T(8,128)}) %all-gather.11.cloned.1.call-update) | async-done | bytes 4194320 | tf_op jit(solution)/shard_map/all_gather | solution.py:20
  638.2 4.6 fusion.5
  642.8 0.7 fusion.19
  643.5 1.5 copy.11
  645.0 0.0 reduce-scatter.3.cloned.1.call-update
  645.0 0.0 reduce-scatter.5.cloned.1.call-start
  645.1 21.5 %reduce-scatter.3.cloned.1.call-done = f32[16,16,1024]{2,1,0:T(8,128)} async-done(((f32[32,16,1024]{2,1,0:T(8,128)}), f32[16,16,1024]{2,1,0:T(8,128)}) %reduce-scatter.3.cloned.1.call-update) | async-done | bytes 1048592 | tf_op jit(solution)/shard_map/reduce_scatter | solution.py:35
  666.6 0.0 reduce-scatter.5.cloned.1.call-update
  666.6 0.0 copy-done.6
  666.6 1.7 convolution_convert_fusion
  668.3 73.1 %reduce-scatter.5.cloned.1.call-done = f32[1,16,1024]{2,1,0:T(8,128)} async-done(((f32[16,16,1024]{2,1,0:T(8,128)}), f32[1,16,1024]{2,1,0:T(8,128)}) %reduce-scatter.5.cloned.1.call-update) | async-done | bytes 65552 | tf_op jit(solution)/shard_map/reduce_scatter | solution.py:35
  741.5 1.5 bitcast_multiply_fusion
  (19 shorter events, 0.1 us)
Async XLA Ops:
  7.2 393.6 %copy-start = (bf16[1024,512]{1,0:T(8,128)(2,1)S(1)}, bf16[1024,512]{1,0:T(8,128)(2,1)}, u32[]{:S(2)}) copy-start(bf16[1024,512]{1,0:T(8,128)(2,1)} %param.9) | copy-start | bytes 3145732
  7.2 3.7 copy-start.7
  7.2 368.3 %all-gather.13.cloned.1.call-start = ((), (), s32[]{:S(2)}) async-start(), calls=%async_computation.6 | async-start | bytes 69206016 | tf_op jit(solution)/shard_map/all_gather | solution.py:72
  10.8 0.7 copy-start.11
  10.8 0.7 copy-start.10
  10.8 445.7 %all-gather.15.cloned.1.call-start = ((), (), s32[]{:S(2)}) async-start(), calls=%async_computation.7 | async-start | bytes 5242880 | tf_op jit(solution)/shard_map/all_gather | solution.py:20
  135.2 262.5 %copy-start.2 = (f32[512,1024]{1,0:T(8,128)}, f32[512,1024]{1,0:T(8,128)S(1)}, u32[]{:S(2)}) copy-start(f32[512,1024]{1,0:T(8,128)S(1)} %reshape.63) | copy-start | bytes 6291460
  375.5 22.2 %copy-start.8 = (f32[1024]{0:T(1024)S(1)}, f32[1024]{0:T(1024)}, u32[]{:S(2)}) copy-start(f32[1024]{0:T(1024)} %param.8) | copy-start | bytes 12292
  399.8 1.0 copy-start.5
  402.5 113.2 %copy-start.3 = (f32[512,512]{1,0:T(8,128)S(1)}, f32[512,512]{1,0:T(8,128)}, u32[]{:S(2)}) copy-start(f32[512,512]{1,0:T(8,128)} %fusion.18) | copy-start | bytes 3145732
  402.5 113.2 %copy-start.4 = (bf16[512,512]{1,0:T(8,128)(2,1)S(1)}, bf16[512,512]{1,0:T(8,128)(2,1)}, u32[]{:S(2)}) copy-start(bf16[512,512]{1,0:T(8,128)(2,1)} %param.6) | copy-start | bytes 1572868
  402.6 113.2 %copy-start.9 = (f32[512]{0:T(512)S(1)}, f32[512]{0:T(512)}, u32[]{:S(2)}) copy-start(f32[512]{0:T(512)} %param.10) | copy-start | bytes 6148
  402.6 113.2 %all-gather.9.cloned.1.call-start = ((), (), s32[]{:S(2)}) async-start(), calls=%async_computation.2 | async-start | bytes 5242880 | tf_op jit(solution)/shard_map/all_gather | solution.py:20
  460.2 118.7 %all-gather.17.cloned.1.call-start = ((), (), s32[]{:S(2)}) async-start(), calls=%async_computation.8 | async-start | bytes 5242880 | tf_op jit(solution)/shard_map/all_gather | solution.py:20
  521.5 116.7 %copy-start.1 = (f32[512,512]{1,0:T(8,128)S(1)}, f32[512,512]{1,0:T(8,128)}, u32[]{:S(2)}) copy-start(f32[512,512]{1,0:T(8,128)} %fusion.12) | copy-start | bytes 3145732
  521.5 116.7 %all-gather.11.cloned.1.call-start = ((), (), s32[]{:S(2)}) async-start(), calls=%async_computation.3 | async-start | bytes 5242880 | tf_op jit(solution)/shard_map/all_gather | solution.py:20
  582.6 84.0 %reduce-scatter.3.cloned.1.call-start = ((), (), s32[]{:S(2)}) async-start(), calls=%async_computation.4 | async-start | bytes 3145728 | tf_op jit(solution)/shard_map/reduce_scatter | solution.py:35
  645.0 21.6 %copy-start.6 = (bf16[512,1024]{1,0:T(8,128)(2,1)S(1)}, bf16[512,1024]{1,0:T(8,128)(2,1)}, u32[]{:S(2)}) copy-start(bf16[512,1024]{1,0:T(8,128)(2,1)} %copy-done.5) | copy-start | bytes 3145732
  645.0 96.4 %reduce-scatter.5.cloned.1.call-start = ((), (), s32[]{:S(2)}) async-start(), calls=%async_computation.5 | async-start | bytes 1114112 | tf_op jit(solution)/shard_map/reduce_scatter | solution.py:35
Sparse Core Ops, SparseCore 0:
  10.9 364.5 all-gather.12
  402.7 53.8 all-gather.14
  460.3 55.3 all-gather.8
  521.6 57.2 all-gather.16
  582.7 55.3 all-gather.10
  645.1 21.3 reduce-scatter.2
  669.6 71.7 reduce-scatter.4
